TPU v7x, 32 devices: a whole 2x2x4 slice. The times are simulated.
32 devices in a mesh: groups: 2 (over x), samp: 16 (over z, y, core).
Axes of the slice: x: 2, y: 2, z: 4, core: 2. Of those that a mesh axis runs over, the one named last changes fastest.
Arguments:
- gradients: bfloat16 [8192, 32768], P(('groups', 'samp')), parts along dimension 0, may hold values from -45 to 45
- sketch: bfloat16 [8192, 128], P(('groups', 'samp')), parts along dimension 0, may hold values from -6 to 6
Outputs:
- basis: float32 [32768, 256], P('samp', 'groups'), parts along dimension 1
- factor: float32 [256, 128], P('groups'), parts along dimension 0
There are 2 independent parts, one for each index of `groups`. A program takes and returns all parts, laid end to end along the dimension named above; each array names one. Nothing has to cross between parts.
All inputs are finite; a program needn't handle non-finite values.
Results may differ from a plain program's by a relative error of at most 0.0029.
Values may be sent and summed in bfloat16 or wider, within the bound.
A program may use at most 128 MiB of HBM per device.

v0:
```python
import jax
import jax.numpy as jnp
from jax import lax
from jax.sharding import PartitionSpec as P

P_SIZE = 32768


def contract_rows(left, right):
    return lax.dot_general(
        left, right, (((0,), (0,)), ((), ())), preferred_element_type=jnp.float32
    )


def local_gram(matrix):
    return (
        lax.dot_general(
            matrix,
            matrix,
            (((0,), (0,)), ((), ())),
            precision=lax.Precision.HIGHEST,
            preferred_element_type=jnp.float32,
        )
        / P_SIZE
    )


def factor_and_apply(gram, matrix):
    lower = jnp.linalg.cholesky(gram)
    identity = jnp.eye(gram.shape[0], dtype=jnp.float32)
    inverse = lax.linalg.triangular_solve(lower, identity, left_side=True, lower=True)
    return (jnp.dot(matrix, inverse.T, precision=lax.Precision.HIGHEST), lower)


def per_device(gradients, sketch):
    rows = gradients.shape[0]
    count = lax.axis_size("samp")
    total = rows * count
    first_full = lax.psum(contract_rows(gradients, sketch), "samp")
    basis_full, unused = factor_and_apply(local_gram(first_full), first_full)
    image = jnp.dot(
        gradients, basis_full.astype(jnp.bfloat16), preferred_element_type=jnp.float32
    ).astype(jnp.bfloat16)
    second_rows = lax.psum_scatter(
        contract_rows(gradients, image) * (1.0 / total), "samp", scatter_dimension=0, tiled=True
    )
    gram_two = lax.psum(local_gram(second_rows), "samp")
    basis, lower = factor_and_apply(gram_two, second_rows)
    return (basis, lower.T)


def solution(mesh):
    placed = (P(("groups", "samp"), None), P(("groups", "samp"), None))
    return jax.shard_map(
        per_device,
        mesh=mesh,
        in_specs=placed,
        out_specs=(P("samp", "groups"), P("groups", None)),
        check_vma=False,
    )
```

profile of v0, /device:TPU:8, one launch (start us, length us, event | category | flops | bytes accessed | tf_op | source)
XLA Modules:
  0.0 734.2 jit_solution(3705783789845195583)
XLA Ops:
  7.2 0.0 copy-start
  7.2 0.0 all-reduce.3.cloned.1.call-start
  7.2 0.8 copy-done
  8.0 16.1 %fusion.11 = f32[32768,128]{1,0:T(8,128)} fusion(bf16[256,32768]{1,0:T(8,128)(2,1)} %param.5, bf16[256,128]{1,0:T(8,128)(2,1)S(1)} %copy-done), kind=kOutput, calls=%fused_computation.27 | convolution fusion | flops 2147483648 | bytes 33619968 | tf_op jit(solution)/shard_map/dot_general | solution.py:10
  24.1 0.0 all-reduce.3.cloned.1.call-update
  24.1 0.0 reduce-scatter.2.cloned.1.call-start
  24.2 299.2 %all-reduce.3.cloned.1.call-done = f32[32768,128]{1,0:T(8,128)} async-done(((f32[32768,128]{1,0:T(8,128)}), f32[32768,128]{1,0:T(8,128)}) %all-reduce.3.cloned.1.call-update) | async-done | bytes 16777232 | tf_op jit(solution)/shard_map/psum | solution.py:39
  323.4 37.2 %convolution_multiply_fusion.2 = f32[128,128]{0,1:T(8,128)S(1)} fusion(f32[32768,128]{1,0:T(8,128)} %all-reduce.3.cloned.1.call-done), kind=kOutput, calls=%fused_computation.5 | convolution fusion | flops 6442467328 | bytes 16842752 | tf_op jit(solution)/shard_map/dot_general | solution.py:17
  360.6 0.1 copy.5
  360.7 11.7 %cholesky.44 = f32[128,128]{1,0:T(8,128)S(1)} custom-call(f32[128,128]{1,0:T(8,128)S(1)} %fusion.9), custom_call_target="Cholesky" | custom-call | tf_op jit(solution)/shard_map/jit(cholesky)/cholesky | solution.py:29
  372.5 0.6 compare_reduce_fusion.1
  373.1 0.7 fusion.5
  373.8 9.8 %custom-call.6 = f32[1,128,128]{1,2,0:T(8,128)S(1)} custom-call(f32[1,128,128]{2,1,0:T(8,128)S(1)} %fusion.5), custom_call_target="InvertDiagBlocksLowerTriangular" | custom-call | tf_op jit(solution)/shard_map/triangular_solve/custom-call.0 | solution.py:31
  383.6 0.3 fusion.3
  383.9 17.1 %convolution_convert_fusion = bf16[32768,128]{1,0:T(8,128)(2,1)} fusion(f32[32768,128]{1,0:T(8,128)} %all-reduce.3.cloned.1.call-done, f32[128,128]{1,0:T(8,128)S(1)} %fusion.3), kind=kOutput, calls=%fused_computation.2 | convolution fusion | flops 6446645248 | bytes 25231360 | tf_op jit(solution)/shard_map/dot_general | solution.py:32
  401.0 13.9 %convolution_convert_fusion.1 = bf16[128,256]{1,0:T(8,128)(2,1)S(1)} fusion(bf16[32768,128]{1,0:T(8,128)(2,1)} %convolution_convert_fusion, bf16[256,32768]{1,0:T(8,128)(2,1)} %param.5), kind=kOutput, calls=%fused_computation.3 | convolution fusion | flops 2147516416 | bytes 25231360 | tf_op jit(solution)/shard_map/dot_general | solution.py:41
  414.9 0.0 copy-start.1
  414.9 14.1 %fusion = f32[32768,128]{0,1:T(8,128)} fusion(bf16[128,256]{1,0:T(8,128)(2,1)S(1)} %convolution_convert_fusion.1, bf16[256,32768]{1,0:T(8,128)(2,1)} %param.5), kind=kOutput, calls=%fused_computation.1 | convolution fusion | flops 2151677952 | bytes 33619968 | tf_op jit(solution)/shard_map/dot_general | solution.py:10
  429.0 0.0 reduce-scatter.2.cloned.1.call-update
  429.0 0.2 all-reduce.5.cloned.1.call-start
  429.2 177.2 %reduce-scatter.2.cloned.1.call-done = f32[2048,128]{0,1:T(8,128)} async-done(((f32[32768,128]{0,1:T(8,128)}), f32[2048,128]{0,1:T(8,128)}) %reduce-scatter.2.cloned.1.call-update) | async-done | bytes 1048592 | tf_op jit(solution)/shard_map/reduce_scatter | solution.py:44
  606.4 3.2 convolution_multiply_fusion.1
  609.6 0.0 all-reduce.5.cloned.1.call-update
  609.7 88.2 %all-reduce.5.cloned.1.call-done = f32[128,128]{0,1:T(8,128)} async-done(((f32[128,128]{0,1:T(8,128)}), f32[128,128]{0,1:T(8,128)}) %all-reduce.5.cloned.1.call-update) | async-done | bytes 65552 | tf_op jit(solution)/shard_map/psum | solution.py:47
  697.8 0.9 copy.7
  698.8 0.9 fusion.7
  699.6 11.7 %cholesky.55 = f32[128,128]{1,0:T(8,128)S(1)} custom-call(f32[128,128]{1,0:T(8,128)S(1)} %fusion.7), custom_call_target="Cholesky" | custom-call | tf_op jit(solution)/shard_map/jit(cholesky)/cholesky | solution.py:29
  711.4 0.6 compare_reduce_fusion
  712.0 0.7 fusion.10
  712.7 0.7 copy.8
  713.4 9.8 %custom-call.7 = f32[1,128,128]{1,2,0:T(8,128)S(1)} custom-call(f32[1,128,128]{2,1,0:T(8,128)S(1)} %get-tuple-element.7), custom_call_target="InvertDiagBlocksLowerTriangular" | custom-call | tf_op jit(solution)/shard_map/triangular_solve/custom-call.0 | solution.py:31
  723.2 0.3 fusion.1
  723.5 4.0 fusion.12
  727.5 0.0 copy-done.1
  (3 shorter events, 0.1 us)
Async XLA Ops:
  7.2 0.8 copy-start
  7.2 316.2 %all-reduce.3.cloned.1.call-start = ((), (), s32[]{:S(2)}) async-start(), calls=%async_computation.1 | async-start | bytes 33554432 | tf_op jit(solution)/shard_map/psum | solution.py:39
  24.1 582.3 %reduce-scatter.2.cloned.1.call-start = ((), (), s32[]{:S(2)}) async-start(), calls=%async_computation.2 | async-start | bytes 17825792 | tf_op jit(solution)/shard_map/reduce_scatter | solution.py:44
  414.9 312.6 %copy-start.1 = (bf16[256,128]{1,0:T(8,128)(2,1)S(1)}, bf16[256,128]{1,0:T(8,128)(2,1)}, u32[]{:S(2)}) copy-start(bf16[256,128]{1,0:T(8,128)(2,1)} %param.6) | copy-start | bytes 196612
  429.0 268.8 %all-reduce.5.cloned.1.call-start = ((), (), s32[]{:S(2)}) async-start(), calls=%async_computation.3 | async-start | bytes 131072 | tf_op jit(solution)/shard_map/psum | solution.py:47
Sparse Core Ops, SparseCore 0:
  24.2 299.0 all-reduce.2
  429.1 177.2 reduce-scatter.1
  610.4 87.3 all-reduce.4
where the time goes:
time: 744 us; the launch traced here: 734 us
  waiting for transfers between devices  565 us (76%)
  matrix products  106 us (14%)
  other arithmetic  46.6 us (6%)
  between operations  14 us (2%)
    psum x1, waiting for transfers between devices, per_device(): first_full = lax.psum(contract_rows(gradients, sketch), 'samp')  299 us
    reduce_scatter x1, waiting for transfers between devices, per_device(): lax.psum_scatter(contract_rows(gradients, image) * (1.0 / total), 'samp',...  177 us
    psum x1, waiting for transfers between devices, per_device(): gram_two = lax.psum(local_gram(second_rows), 'samp')  88.2 us
    dot_general x2, matrix products, local_gram(): lax.dot_general(matrix, matrix, (((0,), (0,)), ((), ())), precision=lax.P...  40.5 us
    dot_general x2, matrix products, contract_rows(): lax.dot_general(left, right, (((0,), (0,)), ((), ())), preferred_element_...  30.2 us
    another operation x6, other arithmetic, factor_and_apply(): lower = jnp.linalg.cholesky(gram)  24.8 us
    dot_general x2, matrix products, factor_and_apply(): return (jnp.dot(matrix, inverse.T, precision=lax.Precision.HIGHEST), lower)  21.1 us
    another operation x3, other arithmetic, factor_and_apply(): lax.linalg.triangular_solve(lower, identity, left_side=True, lower=True)  20.3 us
  transfers between devices with their start and end apart: 3, of which 3 were waited for; matrix products, arithmetic and copies ran while one was open for 0% of the time, Pallas kernels for 0%

commit v1 on v0

v1 whole, which is shorter than its diff:
```python
import functools

import jax
import jax.numpy as jnp
from jax import lax
from jax.experimental import pallas as pl
from jax.experimental.pallas import tpu as pltpu
from jax.sharding import PartitionSpec as P

MESH = pl.DeviceIdType.MESH
SUB = 2
MIB = 1024 * 1024


def position(nz):
    me = lax.axis_index("samp")
    return lax.div(me, 4), lax.rem(lax.div(me, 2), 2), lax.rem(me, 2)


def place(z, y, c):
    return (lax.axis_index("groups"), z * 4 + y * 2 + c)


def outward(nz, z, k):
    mirror = z >= nz - z
    zm = jnp.where(mirror, nz - 1 - z, z)
    base = nz - 1 - 2 * zm
    kk = jnp.maximum(k - base, 0)
    half = lax.div(kk, 2)
    inner = jnp.where(lax.rem(kk, 2) == 0, half, 2 * zm - half)
    at = jnp.where(k < base, nz - 1 - k, inner)
    return jnp.where(mirror, nz - 1 - at, at)


def enter(nz, z, y, c):
    barrier = pltpu.get_barrier_semaphore()
    pl.semaphore_signal(barrier, inc=1, device_id=place(z, y, 1 - c), device_id_type=MESH)
    pl.semaphore_signal(barrier, inc=1, device_id=place(z, 1 - y, c), device_id_type=MESH)
    for o in range(1, nz):
        pl.semaphore_signal(
            barrier, inc=1, device_id=place(lax.rem(z + o, nz), y, c), device_id_type=MESH
        )
    pl.semaphore_wait(barrier, nz + 1)


def remote(src, dst, send, recv, to):
    return pltpu.make_async_remote_copy(
        src_ref=src, dst_ref=dst, send_sem=send, recv_sem=recv, device_id=to, device_id_type=MESH
    )


def product(own_lhs, other_lhs, own, other, idx):
    return jnp.dot(own_lhs, own[idx], preferred_element_type=jnp.float32) + jnp.dot(
        other_lhs, other[idx], preferred_element_type=jnp.float32
    )


def reduce_scatter(nz, z, y, c, partial, acc, ysend, yrecv, zsend, zrecv, sems, wide=None):
    ys, yr, zs, zr = sems

    @pl.loop(0, nz * SUB)
    def send_pair(t):
        k, h = lax.div(t, SUB), lax.rem(t, SUB)
        zd = outward(nz, z, k)
        slot = zd * SUB + h
        ysend[slot] = partial((zd * 2 + 1 - y) * SUB + h).astype(jnp.bfloat16)
        remote(
            ysend.at[slot], yrecv.at[slot], ys.at[slot], yr.at[slot], place(z, 1 - y, c)
        ).start()

    def y_copy(slot):
        return remote(
            ysend.at[slot], yrecv.at[slot], ys.at[slot], yr.at[slot], place(z, 1 - y, c)
        )

    def z_copy(slot, into, to):
        return remote(zsend.at[slot], zrecv.at[into], zs.at[slot], zr.at[into], place(to, y, c))

    def w_copy(slot, to):
        return remote(
            wide[0].at[slot], wide[1].at[slot], wide[2].at[slot], wide[3].at[slot],
            place(to, y, c),
        )

    @pl.loop(0, nz * SUB)
    def along(t):
        k, h = lax.div(t, SUB), lax.rem(t, SUB)
        zd = outward(nz, z, k)
        slot = zd * SUB + h
        acc[h] = partial((zd * 2 + y) * SUB + h)
        y_copy(slot).wait_recv()
        acc[h] += yrecv[slot].astype(jnp.float32)

        from_left_wide = jnp.logical_and(zd == z, z > 1)
        from_right_wide = jnp.logical_and(zd == z, z < nz - 2)
        to_right_wide = jnp.logical_and(zd == z + 1, z > 0)
        to_left_wide = jnp.logical_and(zd == z - 1, z < nz - 1)
        from_left, from_right = jnp.logical_and(zd >= z, z > 0), jnp.logical_and(zd <= z, z < nz - 1)
        to_right, to_left = zd > z, zd < z
        if wide is not None:
            for side, arrives in enumerate((from_left_wide, from_right_wide)):

                @pl.when(arrives)
                def take_wide():
                    w_copy(side * SUB + h, z).wait_recv()
                    acc[h] += wide[1][side * SUB + h]

            from_left = jnp.logical_and(from_left, jnp.logical_not(from_left_wide))
            from_right = jnp.logical_and(from_right, jnp.logical_not(from_right_wide))
            to_right = jnp.logical_and(to_right, jnp.logical_not(to_right_wide))
            to_left = jnp.logical_and(to_left, jnp.logical_not(to_left_wide))

        @pl.when(from_left)
        def take_left():
            z_copy(slot, slot, z).wait_recv()
            acc[h] += zrecv[slot].astype(jnp.float32)

        right = jnp.where(zd == z, nz, zd) * SUB + h

        @pl.when(from_right)
        def take_right():
            z_copy(slot, right, z).wait_recv()
            acc[h] += zrecv[right].astype(jnp.float32)

        if wide is not None:
            for side, (leaves, to) in enumerate(((to_right_wide, z + 1), (to_left_wide, z - 1))):

                @pl.when(leaves)
                def give_wide():
                    wide[0][side * SUB + h] = acc[h]
                    w_copy(side * SUB + h, to).start()

        @pl.when(to_right)
        def give_right():
            zsend[slot] = acc[h].astype(jnp.bfloat16)
            z_copy(slot, slot, z + 1).start()

        @pl.when(to_left)
        def give_left():
            zsend[slot] = acc[h].astype(jnp.bfloat16)
            z_copy(slot, jnp.where(zd == z - 1, nz, zd) * SUB + h, z - 1).start()

    @pl.loop(0, nz * SUB)
    def sent(t):
        y_copy(t).wait_send()

        zd, h = lax.div(t, SUB), lax.rem(t, SUB)
        narrow = zd != z
        if wide is not None:
            for side, zw in enumerate((z + 1, z - 1)):
                leaves = jnp.logical_and(zd == zw, (z > 0) if side == 0 else (z < nz - 1))

                @pl.when(leaves)
                def wide_sent():
                    w_copy(side * SUB + h, z).wait_send()

                narrow = jnp.logical_and(narrow, jnp.logical_not(leaves))

        @pl.when(narrow)
        def line_sent():
            z_copy(t, t, z).wait_send()


def first_kernel(
    nz, g_ref, s_ref, img_ref, gram_ref, keep_ref,
    own, other, s_other, acc, ysend, yrecv, zsend, zrecv, full, give, take,
    ys, yr, zs, zr, load, gs, gr, store, ss, ar, al, ay, arz, ary, xs,
):
    z, y, c = position(nz)
    width = own.shape[2]
    enter(nz, z, y, c)
    sibling = place(z, y, 1 - c)

    def columns(idx, core):
        p, h = lax.div(idx, SUB), lax.rem(idx, SUB)
        return pl.ds(pl.multiple_of(((p * 2 + core) * SUB + h) * width, width), width)

    def mine(idx):
        return pltpu.make_async_copy(g_ref.at[:, columns(idx, c)], own.at[idx], load.at[idx])

    def swap(idx):
        return remote(
            g_ref.at[:, columns(idx, 1 - c)], other.at[idx], gs.at[idx], gr.at[idx], sibling
        )

    def put(idx):
        return pltpu.make_async_copy(other.at[idx], keep_ref.at[idx], store.at[idx])

    sketch_copy = remote(s_ref, s_other, ss.at[0], ss.at[1], sibling)
    sketch_copy.start()
    for pair in (1, 0):

        @pl.loop(0, nz * SUB)
        def begin(t):
            zd = outward(nz, z, lax.div(t, SUB))
            yd = 1 - y if pair else y
            idx = (zd * 2 + yd) * SUB + lax.rem(t, SUB)
            swap(idx).start()
            mine(idx).start()

    sketch_copy.wait()

    def partial(idx):
        mine(idx).wait()
        swap(idx).wait_recv()
        put(idx).start()
        return product(s_ref[...], s_other[...], own, other, idx)

    reduce_scatter(nz, z, y, c, partial, acc, ysend, yrecv, zsend, zrecv, (ys, yr, zs, zr))

    give[...] = jnp.zeros_like(give)

    def block(zz, yy, h):
        return full.at[(zz * 2 + yy) * SUB + h]

    def g_right(zz, h):
        s = zz * SUB + h
        return remote(block(zz, y, h), block(zz, y, h), ar.at[s], arz.at[s], place(z + 1, y, c))

    def g_left(zz, h):
        s = zz * SUB + h
        return remote(block(zz, y, h), block(zz, y, h), al.at[s], arz.at[s], place(z - 1, y, c))

    def g_pair(zz, h):
        s = zz * SUB + h
        return remote(block(zz, y, h), block(zz, y, h), ay.at[s], ary.at[s], place(z, 1 - y, c))

    def from_pair(zz, h):
        s = zz * SUB + h
        return remote(
            block(zz, 1 - y, h), block(zz, 1 - y, h), ay.at[s], ary.at[s], place(z, 1 - y, c)
        )

    def use(idx):
        got = full[idx]
        rows = own.shape[1]
        give[:, rows : 2 * rows] += lax.dot_general(
            got, own[idx], (((1,), (1,)), ((), ())), preferred_element_type=jnp.float32
        )
        give[:, 0:rows] += lax.dot_general(
            got, other[idx], (((1,), (1,)), ((), ())), preferred_element_type=jnp.float32
        )
        give[:, 2 * rows :] += lax.dot_general(
            got, got, (((1,), (1,)), ((), ())), preferred_element_type=jnp.float32
        )

    def goes_right(zz):
        return jnp.logical_and(zz <= z, z < nz - 1)

    def goes_left(zz):
        return jnp.logical_and(zz >= z, z > 0)

    @pl.loop(0, nz * SUB)
    def line(t):
        k, h = lax.div(t, SUB), lax.rem(t, SUB)
        zz = outward(nz, z, nz - 1 - k)

        @pl.when(k == 0)
        def local():
            full[(z * 2 + y) * SUB + h] = acc[h].astype(jnp.bfloat16)

        @pl.when(k > 0)
        def arrived():
            g_right(zz, h).wait_recv()

        @pl.when(goes_right(zz))
        def right():
            g_right(zz, h).start()

        @pl.when(goes_left(zz))
        def left():
            g_left(zz, h).start()

        g_pair(zz, h).start()
        use((zz * 2 + y) * SUB + h)

    @pl.loop(0, nz * SUB)
    def pair_blocks(t):
        k, h = lax.div(t, SUB), lax.rem(t, SUB)
        zz = outward(nz, z, nz - 1 - k)
        from_pair(zz, h).wait_recv()
        use((zz * 2 + 1 - y) * SUB + h)

    exchange = remote(give, take, xs.at[0], xs.at[1], sibling)
    exchange.start()

    @pl.loop(0, nz * SUB)
    def sent(t):
        zz, h = lax.div(t, SUB), lax.rem(t, SUB)
        g_pair(zz, h).wait_send()

        @pl.when(goes_right(zz))
        def right():
            g_right(zz, h).wait_send()

        @pl.when(goes_left(zz))
        def left():
            g_left(zz, h).wait_send()

    @pl.loop(0, 2 * nz * SUB)
    def stored(t):
        put(t).wait()
        swap(t).wait_send()

    exchange.wait()
    rows = own.shape[1]
    img_ref[0] = give[:, rows : 2 * rows] + take[:, 0:rows]
    img_ref[1] = give[:, 0:rows] + take[:, rows : 2 * rows]
    gram_ref[...] = give[:, 2 * rows :] + take[:, 2 * rows :]


def second_kernel(
    nz, scale, inv_p, g_ref, keep_ref, img_ref, inv_ref, second_ref, gram_ref,
    own, other, image, acc, ysend, yrecv, zsend, zrecv, part, pair_in, line_in,
    wsend, wrecv, ys, yr, zs, zr, load, fetch, xs, vs, ws, wr,
):
    z, y, c = position(nz)
    width = own.shape[2]

    def mine(idx):
        p, h = lax.div(idx, SUB), lax.rem(idx, SUB)
        at = pl.ds(pl.multiple_of(((p * 2 + c) * SUB + h) * width, width), width)
        return pltpu.make_async_copy(g_ref.at[:, at], own.at[idx], load.at[idx])

    def kept(idx):
        return pltpu.make_async_copy(keep_ref.at[idx], other.at[idx], fetch.at[idx])

    for pair in (1, 0):

        @pl.loop(0, nz * SUB)
        def begin(t):
            zd = outward(nz, z, lax.div(t, SUB))
            yd = 1 - y if pair else y
            idx = (zd * 2 + yd) * SUB + lax.rem(t, SUB)
            mine(idx).start()
            kept(idx).start()

    enter(nz, z, y, c)
    for side in range(2):
        image[side] = jnp.dot(
            inv_ref[...], img_ref[side],
            precision=lax.Precision.HIGHEST, preferred_element_type=jnp.float32,
        ).astype(jnp.bfloat16)

    def partial(idx):
        mine(idx).wait()
        kept(idx).wait()
        return product(image[0], image[1], own, other, idx)

    reduce_scatter(
        nz, z, y, c, partial, acc, ysend, yrecv, zsend, zrecv, (ys, yr, zs, zr),
        (wsend, wrecv, ws, wr),
    )
    total = jnp.zeros(part.shape[1:], jnp.float32)
    for h in range(SUB):
        rows = acc[h] * scale
        second_ref[:, h * width : (h + 1) * width] = rows
        total = total + lax.dot_general(
            rows, rows, (((1,), (1,)), ((), ())),
            precision=lax.Precision.HIGHEST, preferred_element_type=jnp.float32,
        )
    part[0] = total * inv_p
    core = remote(part.at[0], pair_in.at[0], xs.at[0], xs.at[1], place(z, y, 1 - c))
    core.start()
    core.wait()
    part[1] = part[0] + pair_in[0]
    across = remote(part.at[1], pair_in.at[1], xs.at[2], xs.at[3], place(z, 1 - y, c))
    across.start()
    across.wait()
    part[2] = part[1] + pair_in[1]

    def line(o):
        return remote(
            part.at[2], line_in.at[o], vs.at[o], vs.at[nz + o], place(lax.rem(z + o, nz), y, c)
        )

    for o in range(1, nz):
        line(o).start()
    line_in[0] = part[2]
    for o in range(1, nz):
        line(o).wait()
    total = jnp.zeros(part.shape[1:], jnp.float32)
    for at in range(nz):
        total = total + line_in[lax.rem(z - at + nz, nz)]
    gram_ref[...] = total


def invert(gram):
    lower = jnp.linalg.cholesky(gram)
    identity = jnp.eye(gram.shape[0], dtype=jnp.float32)
    return lower, lax.linalg.triangular_solve(lower, identity, left_side=True, lower=True)


def per_device(gradients, sketch):
    rows, params = gradients.shape
    cols = sketch.shape[1]
    n = lax.axis_size("samp")
    nz = n // 4
    share = params // n
    width = share // SUB
    blocks = 2 * nz * SUB
    line = nz * SUB
    f32, bf16 = jnp.float32, jnp.bfloat16
    anywhere = pl.BlockSpec(memory_space=pl.ANY)
    vmem = pl.BlockSpec(memory_space=pltpu.VMEM)
    dma = pltpu.SemaphoreType.DMA
    limit = 48 * MIB
    reduce_buffers = [
        pltpu.VMEM((SUB, cols, width), f32),
        pltpu.VMEM((line, cols, width), bf16),
        pltpu.VMEM((line, cols, width), bf16),
        pltpu.VMEM((line, cols, width), bf16),
        pltpu.VMEM((line + SUB, cols, width), bf16),
    ]
    reduce_sems = [dma((line,)), dma((line,)), dma((line,)), dma((line + SUB,))]
    img, gram_one, keep = pl.pallas_call(
        functools.partial(first_kernel, nz),
        out_shape=(
            jax.ShapeDtypeStruct((2, cols, rows), f32),
            jax.ShapeDtypeStruct((cols, cols), f32),
            jax.ShapeDtypeStruct((blocks, rows, width), bf16),
        ),
        in_specs=[anywhere, vmem],
        out_specs=(vmem, vmem, anywhere),
        scratch_shapes=[
            pltpu.VMEM((blocks, rows, width), bf16),
            pltpu.VMEM((blocks, rows, width), bf16),
            pltpu.VMEM((cols, rows), bf16),
            *reduce_buffers,
            pltpu.VMEM((blocks, cols, width), bf16),
            pltpu.VMEM((cols, 2 * rows + cols), f32),
            pltpu.VMEM((cols, 2 * rows + cols), f32),
            *reduce_sems,
            dma((blocks,)), dma((blocks,)), dma((blocks,)), dma((blocks,)), dma((2,)),
            dma((line,)), dma((line,)), dma((line,)), dma((line,)), dma((line,)), dma((2,)),
        ],
        compiler_params=pltpu.CompilerParams(
            collective_id=0, has_side_effects=True, vmem_limit_bytes=limit
        ),
        name="first_pass",
    )(gradients, sketch.T)
    unused, inverse_one = invert(gram_one / params)
    second, gram_two = pl.pallas_call(
        functools.partial(second_kernel, nz, 1.0 / (rows * n), 1.0 / params),
        out_shape=(
            jax.ShapeDtypeStruct((cols, share), f32),
            jax.ShapeDtypeStruct((cols, cols), f32),
        ),
        in_specs=[anywhere, anywhere, vmem, vmem],
        out_specs=(vmem, vmem),
        scratch_shapes=[
            pltpu.VMEM((blocks, rows, width), bf16),
            pltpu.VMEM((blocks, rows, width), bf16),
            pltpu.VMEM((2, cols, rows), bf16),
            *reduce_buffers,
            pltpu.VMEM((3, cols, cols), f32),
            pltpu.VMEM((2, cols, cols), f32),
            pltpu.VMEM((nz, cols, cols), f32),
            pltpu.VMEM((2 * SUB, cols, width), f32),
            pltpu.VMEM((2 * SUB, cols, width), f32),
            *reduce_sems,
            dma((blocks,)), dma((blocks,)), dma((4,)), dma((2 * nz,)), dma((2 * SUB,)), dma((2 * SUB,)),
        ],
        compiler_params=pltpu.CompilerParams(
            collective_id=1, has_side_effects=True, vmem_limit_bytes=limit
        ),
        name="second_pass",
    )(gradients, keep, img, inverse_one)
    lower, inverse_two = invert(gram_two)
    basis = lax.dot_general(
        second, inverse_two, (((0,), (1,)), ((), ())),
        precision=lax.Precision.HIGHEST, preferred_element_type=f32,
    )
    return (basis, lower.T)


def solution(mesh):
    placed = (P(("groups", "samp"), None), P(("groups", "samp"), None))
    return jax.shard_map(
        per_device,
        mesh=mesh,
        in_specs=placed,
        out_specs=(P("samp", "groups"), P("groups", None)),
        check_vma=False,
    )
```

time: 744 us -> 224 us (0.30)
  waiting for transfers between devices: 565 us -> 0 us
  Pallas kernels: 0 us -> 170 us
  matrix products: 106 us -> 3.35 us
  between operations: 14 us -> 0.75 us
    psum x2 -> x0, waiting for transfers between devices: 387 us -> none  [the longest x1 299 us: per_device(): first_full = lax.psum(contract_rows(gradients, sketch), 'samp')]
    reduce_scatter x1 -> x0, waiting for transfers between devices: 177 us -> none  [per_device(): lax.psum_scatter(contract_rows(gradients, image) * (1.0 / total), 'samp',...]
    pallas_call x0 -> x2, Pallas kernels: none -> 170 us  [the longest x1 102 us: per_device(): pl.pallas_call(functools.partial(first_kernel, nz), out_shape=(jax.ShapeD...]
    dot_general x7 -> x1, matrix products: 106 us -> 2.78 us  [per_device(): lax.dot_general(second, inverse_two, (((0,), (1,)), ((), ())), precision=...]
  transfers between devices with their start and end apart: 3 -> 0, of which waited for: 3 -> 0; matrix products, arithmetic and copies ran while one was open for 0% -> 0% of each run, Pallas kernels for 0% -> 0%
where the time goes in v1:
time: 224 us; the launch traced here: 221 us
  Pallas kernels  170 us (76%)
  other arithmetic  45.7 us (20%)
  matrix products  3.35 us (1%)
    pallas_call x1, Pallas kernels, per_device(): pl.pallas_call(functools.partial(first_kernel, nz), out_shape=(jax.ShapeD...  102 us
    pallas_call x1, Pallas kernels, per_device(): pl.pallas_call(functools.partial(second_kernel, nz, 1.0 / (rows * n), 1.0...  67.9 us
    another operation x6, other arithmetic, invert(): lower = jnp.linalg.cholesky(gram)  24.8 us
    another operation x3, other arithmetic, invert(): lax.linalg.triangular_solve(lower, identity, left_side=True, lower=True)  20.3 us

profile of v1, /device:TPU:8, one launch (start us, length us, event | category | flops | bytes accessed | tf_op | source)
XLA Modules:
  0.0 221.5 jit_solution(17004433295129483237)
XLA Ops:
  0.6 0.9 copy.4
  1.6 101.8 %first_pass.1 = (f32[2,128,256]{2,1,0:T(8,128)S(1)}, f32[128,128]{1,0:T(8,128)S(1)}, bf16[16,256,1024]{2,1,0:T(8,128)(2,1)}) custom-call(bf16[256,32768]{1,0:T(8,128)(2,1)} %g_ref.3, bf16[128,256]{1,0:T(8,128)(2,1)S(1)} %bitcast.23), custom_call_target="tpu_custom_call" | custom-call | tf_op jit(solution)/shard_map/first_pass/pallas_call | solution.py:416
  103.4 0.1 copy.5
  103.5 0.1 copy.6
  103.6 11.7 %cholesky.44 = f32[128,128]{1,0:T(8,128)S(1)} custom-call(f32[128,128]{1,0:T(8,128)S(1)} %fusion.8), custom_call_target="Cholesky" | custom-call | tf_op jit(solution)/shard_map/jit(cholesky)/cholesky | solution.py:389
  115.4 0.6 compare_reduce_fusion.1
  116.0 0.7 fusion.4
  116.7 9.8 %custom-call.6 = f32[1,128,128]{1,2,0:T(8,128)S(1)} custom-call(f32[1,128,128]{2,1,0:T(8,128)S(1)} %fusion.4), custom_call_target="InvertDiagBlocksLowerTriangular" | custom-call | tf_op jit(solution)/shard_map/triangular_solve/custom-call.0 | solution.py:391
  126.5 0.3 fusion.2.inv_ref
  126.8 67.9 %second_pass.1 = (f32[128,2048]{1,0:T(8,128)S(1)}, f32[128,128]{1,0:T(8,128)S(1)}) custom-call(bf16[256,32768]{1,0:T(8,128)(2,1)} %g_ref.3, bf16[16,256,1024]{2,1,0:T(8,128)(2,1)} %get-tuple-element.9.keep_ref, f32[2,128,256]{2,1,0:T(8,128)S(1)} %get-tuple-element.10.img_ref, f32[128,128]{1,0:T(8,128)S(1)} %fusion.2.inv_ref), custom_call_target="tpu_custom_call" | custom-call | tf_op jit(solution)/shard_map/second_pass/pallas_call | solution.py:443
  194.7 0.1 copy.7
  194.8 11.7 %cholesky.55 = f32[128,128]{1,0:T(8,128)S(1)} custom-call(f32[128,128]{1,0:T(8,128)S(1)} %fusion.6), custom_call_target="Cholesky" | custom-call | tf_op jit(solution)/shard_map/jit(cholesky)/cholesky | solution.py:389
  206.5 0.6 compare_reduce_fusion
  207.2 0.7 fusion.9
  207.9 0.7 copy.8
  208.6 9.8 %custom-call.7 = f32[1,128,128]{1,2,0:T(8,128)S(1)} custom-call(f32[1,128,128]{2,1,0:T(8,128)S(1)} %get-tuple-element.17), custom_call_target="InvertDiagBlocksLowerTriangular" | custom-call | tf_op jit(solution)/shard_map/triangular_solve/custom-call.0 | solution.py:391
  218.4 0.3 fusion
  218.7 2.8 %fusion.10 = f32[2048,128]{1,0:T(8,128)} fusion(f32[128,2048]{1,0:T(8,128)S(1)} %get-tuple-element.12, f32[128,128]{1,0:T(8,128)S(1)} %fusion), kind=kOutput, calls=%fused_computation.22 | convolution fusion | flops 402653184 | bytes 2162688 | tf_op jit(solution)/shard_map/dot_general | solution.py:470
  (5 shorter events, 0.1 us)
